TPU v7x, 512 devices: a whole 4x8x8 slice. The times are simulated.
512 devices in a mesh: dir: 16 (over y, x_lo), space: 32 (over z, x_hi, core).
Axes of the slice: x: 4 (x_hi: 2, x_lo: 2; x = x_hi * 2 + x_lo), y: 8, z: 8, core: 2. Of those that a mesh axis runs over, the one named last changes fastest.
Arguments:
- velocity: float32 [16, 3, 256, 16, 512], P('dir', None, 'space'), may hold values from -6 to 6
- precursor: float32 [16, 3, 256, 512], P('dir', None, 'space'), may hold values from -6 to 6
- rot_map: int32 [16, 256, 512], P('dir', 'space'), may hold values from 0 to 131071, as said below
- facade_cell: int32 [16, 8192], P('dir', 'space'), may hold values from 0 to 65535
- facade_owner: int32 [16, 8192, 1], P('dir', 'space'), may hold values from 0 to 31; in each aligned block of 256 rows (0 to 255, 256 to 511, ..., all dimensions but the last counted through in order) at most 24 rows name the same one
- facade_panel: int32 [16, 8192], P('dir', 'space'), may hold values from 0 to 127
- facade_area: float32 [16, 8192], P('dir', 'space'), may hold values from 0.2 to 2
Outputs:
- velocity_new: float32 [16, 3, 256, 16, 512], P('dir', None, 'space')
- potential: float32 [16, 256, 16, 512], P('dir', 'space')
- panel_force: float32 [16, 4096], P('dir', 'space')
Inputs may be any that keep to these rules, and one draw needn't show every extreme that they name: rot_map[d, y, z] = q_d(y) * 512 + z, where q_d is a permutation of the 256 spanwise rows, drawn for each direction. `facade_owner`: among the 256 facade cells of one device at most 24 have the same owner.
All inputs are finite; a program needn't handle non-finite values.
Results may differ from a plain program's by a relative error of at most 0.00002.
Values sent between devices are 32-bit elements; how exact they have to be, the bound alone decides.
A program may use at most 192 MiB of HBM per device.

v0:
```python
import jax
import jax.numpy as jnp
from jax import lax
from jax.sharding import PartitionSpec as P

ITERS = 20
PAN_DEV = 128
time_step = 0.12
viscosity = 0.2


def extended_2(cells, sides, width):
    for axis, dim in sides:
        count = lax.axis_size(axis)
        ends = count - 1
        head = lax.slice_in_dim(cells, 0, width, axis=dim)
        tail = lax.slice_in_dim(cells, cells.shape[dim] - width, cells.shape[dim], axis=dim)
        cells = jnp.concatenate(
            [
                lax.ppermute(tail, axis, [(i, (i + 1) % count) for i in range(ends)]),
                cells,
                lax.ppermute(head, axis, [((i + 1) % count, i) for i in range(ends)]),
            ],
            axis=dim,
        )
    return cells


def spread(block, axis, holder):
    block = jnp.where(lax.axis_index(axis) == holder, block, jnp.zeros_like(block))
    return lax.psum(block, axis)


def pad_edges(field):
    lead = field.ndim - 3
    widths = [(0, 0)] * lead
    padded = jnp.pad(field, widths + [(0, 0), (0, 0), (1, 1)])
    return jnp.pad(padded, widths + [(0, 0), (1, 1), (0, 0)], mode="edge")


def tentative(extended):
    q = pad_edges(extended)
    centre = q[:, 1:-1, 1:-1, 1:-1]
    xplus = q[:, 1:-1, 2:, 1:-1]
    xminus = q[:, 1:-1, :-2, 1:-1]
    zplus = q[:, 1:-1, 1:-1, 2:]
    zminus = q[:, 1:-1, 1:-1, :-2]
    yplus = q[:, 2:, 1:-1, 1:-1]
    yminus = q[:, :-2, 1:-1, 1:-1]
    lap = xplus + xminus + zplus + zminus + 16.0 * (yplus + yminus) - 36.0 * centre
    advect = (
        centre[0] * (xplus - xminus) * 0.5
        + centre[1] * (yplus - yminus) * 2.0
        + centre[2] * (zplus - zminus) * 0.5
    )
    return centre + time_step * (viscosity * lap - advect)


def divergence(extended):
    q = pad_edges(extended)
    along_x = (q[0, 1:-1, 2:, 1:-1] - q[0, 1:-1, :-2, 1:-1]) * 0.5
    along_y = (q[1, 2:, 1:-1, 1:-1] - q[1, :-2, 1:-1, 1:-1]) * 2.0
    along_z = (q[2, 1:-1, 1:-1, 2:] - q[2, 1:-1, 1:-1, :-2]) * 0.5
    return along_x + along_y + along_z


def relax_sweep(extended, source):
    q = jnp.pad(extended, ((0, 0), (1, 1), (1, 1)))
    total = q[1:-1, 2:, 1:-1] + q[1:-1, :-2, 1:-1] + q[1:-1, 1:-1, 2:] + q[1:-1, 1:-1, :-2]
    total = total + 16.0 * (q[2:, 1:-1, 1:-1] + q[:-2, 1:-1, 1:-1])
    return (total - source) / 36.0


def gradient(extended):
    q = jnp.pad(extended, ((0, 0), (1, 1), (1, 1)))
    grad_x = (q[1:-1, 2:, 1:-1] - q[1:-1, :-2, 1:-1]) * 0.5
    grad_y = (q[2:, 1:-1, 1:-1] - q[:-2, 1:-1, 1:-1]) * 2.0
    grad_z = (q[1:-1, 1:-1, 2:] - q[1:-1, 1:-1, :-2]) * 0.5
    return jnp.stack([grad_x, grad_y, grad_z])


def extend(field, width):
    return extended_2(field, (("space", 0),), width)


def inside_rows(first, count, span):
    global_rows = first + jnp.arange(count, dtype=jnp.int32)
    return (global_rows >= 0) & (global_rows < span)


def body(velocity, precursor, rot_map, facade_cell, facade_owner, facade_panel, facade_area):
    groups = lax.axis_size("space")
    rows = velocity.shape[2]
    stream = velocity.shape[3]
    height = velocity.shape[4]
    span = rows * groups
    start = lax.axis_index("space") * rows
    plane_piece = spread(precursor, "dir", 0)
    plane = lax.all_gather(plane_piece[0], "space", axis=1, tiled=True)
    flat_plane = plane.reshape(3, span * height)
    inflow = jnp.take(flat_plane, rot_map[0].reshape(-1), axis=1).reshape(3, rows, height)
    field = velocity[0].at[:, :, 0, :].set(inflow)
    sweeps_each = 1
    widened = extended_2(field, (("space", 1),), sweeps_each + 1)
    ustar_wide = tentative(widened)
    keep = inside_rows(start - sweeps_each, rows + 2 * sweeps_each, span)
    ustar_wide = jnp.where(keep[None, :, None, None], ustar_wide, 0.0)
    ustar = ustar_wide[:, sweeps_each : sweeps_each + rows]
    source_wide = divergence(ustar_wide)
    empty = jnp.zeros((rows, stream, height), jnp.float32)

    def one_round(step, phi):
        current = extend(phi, sweeps_each)
        current = relax_sweep(current, source_wide)
        return current

    phi = lax.fori_loop(0, ITERS // sweeps_each, one_round, empty)
    moved = ustar - gradient(extend(phi, 1))
    values = facade_area[0] * phi.reshape(-1)[facade_cell[0]]
    owners = facade_owner[0, :, 0]
    panels = facade_panel[0]
    panel_count = PAN_DEV
    terms = (
        jnp.zeros((groups * panel_count,), jnp.float32)
        .at[owners * panel_count + panels]
        .add(values)
    )
    force = lax.psum_scatter(terms, "space", scatter_dimension=0, tiled=True)
    return (moved[None], phi[None], force[None])


def solution(mesh):
    return jax.shard_map(
        body,
        mesh=mesh,
        in_specs=(
            P("dir", None, "space", None, None),
            P("dir", None, "space", None),
            P("dir", "space", None),
            P("dir", "space"),
            P("dir", "space", None),
            P("dir", "space"),
            P("dir", "space"),
        ),
        out_specs=(
            P("dir", None, "space", None, None),
            P("dir", "space", None, None),
            P("dir", "space"),
        ),
        check_vma=False,
    )
```

profile of v0, /device:TPU:264, one launch (start us, length us, event | category | flops | bytes accessed | tf_op | source)
XLA Modules:
  0.0 643.1 jit_solution(17695690492703726004)
XLA Ops:
  8.0 62.6 %psum.7 = f32[3,8,512]{2,1,0:T(8,128)} all-reduce(f32[3,8,512]{2,1,0:T(8,128)S(1)} %select_bitcast_fusion), channel_id=1, replica_groups=mesh['dir'=16,'space'=32] {'dir'}, use_global_device_ids=true, to_apply=%region_0.1 | all-reduce | flops 12288 | bytes 98304 | tf_op jit(solution)/shard_map/psum | solution.py:31
  72.7 80.0 %all-gather.2.cloned.1.call-done = f32[3,256,512]{2,1,0:T(8,128)} async-done(((f32[3,8,512]{2,1,0:T(8,128)}), f32[3,256,512]{2,1,0:T(8,128)}) %all-gather.2.cloned.1.call-update) | async-done | bytes 1572880 | tf_op jit(solution)/shard_map/all_gather | solution.py:99
  152.7 32.7 %copy.14 = f32[3,256,512]{0,2,1:T(8,128)} copy(f32[3,256,512]{2,1,0:T(8,128)} %all-gather.2.cloned.1.call-done) | data formatting | bytes 3145728 | tf_op jit(solution)/shard_map/all_gather | solution.py:99
  185.4 60.0 %gather_fusion = f32[4096,3]{1,0:T(8,128)} fusion(f32[3,131072]{0,1:T(8,128)} %bitcast.3, s32[4096]{0:T(1024)S(1)} %broadcast_clamp_fusion), kind=kCustom, calls=%fused_computation | custom fusion | bytes 114688 | tf_op jit(solution)/shard_map/jit(_take)/gather | solution.py:101
  264.6 227.4 %while.14 = (s32[]{:T(128)}, f32[8,16,512]{2,1,0:T(8,128)S(1)}, f32[8,16,512]{2,1,0:T(8,128)S(1)}, s32[]{:T(128)}, s32[]{:T(128)}) while((s32[]{:T(128)}, f32[8,16,512]{2,1,0:T(8,128)S(1)}, f32[8,16,512]{2,1,0:T(8,128)S(1)}, s32[]{:T(128)}, s32[]{:T(128)}) %tuple.48), condition=%wide.region_2.3_spmd.clone, body=%wide.region_1.2_spmd.clone.sunk | while | flops 2108699 | bytes 3515959 | solution.py:117
  266.8 7.3 %collective-permute-start.1 = (f32[1,16,512]{2,1,0:T(8,128)S(1)}, f32[1,16,512]{2,1,0:T(8,128)S(1)}, u32[]{:S(2)}, u32[]{:S(2)}) collective-permute-start(f32[1,16,512]{2,1,0:T(8,128)S(1)} %get-tuple-element.112), channel_id=1, source_target_pairs={{1,0},{2,1},{3,2},{4,3},{5,4},{6,5},{7,6},{8,7},{9,8},{10,9},{11,1... | collective-permute-start | bytes 98312 | tf_op jit(solution)/shard_map/while/body/eval_jaxpr/ppermute | solution.py:22
  278.1 7.3 %collective-permute-start.1 = (f32[1,16,512]{2,1,0:T(8,128)S(1)}, f32[1,16,512]{2,1,0:T(8,128)S(1)}, u32[]{:S(2)}, u32[]{:S(2)}) collective-permute-start(f32[1,16,512]{2,1,0:T(8,128)S(1)} %get-tuple-element.112), channel_id=1, source_target_pairs={{1,0},{2,1},{3,2},{4,3},{5,4},{6,5},{7,6},{8,7},{9,8},{10,9},{11,1... | collective-permute-start | bytes 98312 | tf_op jit(solution)/shard_map/while/body/eval_jaxpr/ppermute | solution.py:22
  289.5 7.3 %collective-permute-start.1 = (f32[1,16,512]{2,1,0:T(8,128)S(1)}, f32[1,16,512]{2,1,0:T(8,128)S(1)}, u32[]{:S(2)}, u32[]{:S(2)}) collective-permute-start(f32[1,16,512]{2,1,0:T(8,128)S(1)} %get-tuple-element.112), channel_id=1, source_target_pairs={{1,0},{2,1},{3,2},{4,3},{5,4},{6,5},{7,6},{8,7},{9,8},{10,9},{11,1... | collective-permute-start | bytes 98312 | tf_op jit(solution)/shard_map/while/body/eval_jaxpr/ppermute | solution.py:22
  300.9 7.3 %collective-permute-start.1 = (f32[1,16,512]{2,1,0:T(8,128)S(1)}, f32[1,16,512]{2,1,0:T(8,128)S(1)}, u32[]{:S(2)}, u32[]{:S(2)}) collective-permute-start(f32[1,16,512]{2,1,0:T(8,128)S(1)} %get-tuple-element.112), channel_id=1, source_target_pairs={{1,0},{2,1},{3,2},{4,3},{5,4},{6,5},{7,6},{8,7},{9,8},{10,9},{11,1... | collective-permute-start | bytes 98312 | tf_op jit(solution)/shard_map/while/body/eval_jaxpr/ppermute | solution.py:22
  312.2 7.3 %collective-permute-start.1 = (f32[1,16,512]{2,1,0:T(8,128)S(1)}, f32[1,16,512]{2,1,0:T(8,128)S(1)}, u32[]{:S(2)}, u32[]{:S(2)}) collective-permute-start(f32[1,16,512]{2,1,0:T(8,128)S(1)} %get-tuple-element.112), channel_id=1, source_target_pairs={{1,0},{2,1},{3,2},{4,3},{5,4},{6,5},{7,6},{8,7},{9,8},{10,9},{11,1... | collective-permute-start | bytes 98312 | tf_op jit(solution)/shard_map/while/body/eval_jaxpr/ppermute | solution.py:22
  323.6 7.3 %collective-permute-start.1 = (f32[1,16,512]{2,1,0:T(8,128)S(1)}, f32[1,16,512]{2,1,0:T(8,128)S(1)}, u32[]{:S(2)}, u32[]{:S(2)}) collective-permute-start(f32[1,16,512]{2,1,0:T(8,128)S(1)} %get-tuple-element.112), channel_id=1, source_target_pairs={{1,0},{2,1},{3,2},{4,3},{5,4},{6,5},{7,6},{8,7},{9,8},{10,9},{11,1... | collective-permute-start | bytes 98312 | tf_op jit(solution)/shard_map/while/body/eval_jaxpr/ppermute | solution.py:22
  334.9 7.3 %collective-permute-start.1 = (f32[1,16,512]{2,1,0:T(8,128)S(1)}, f32[1,16,512]{2,1,0:T(8,128)S(1)}, u32[]{:S(2)}, u32[]{:S(2)}) collective-permute-start(f32[1,16,512]{2,1,0:T(8,128)S(1)} %get-tuple-element.112), channel_id=1, source_target_pairs={{1,0},{2,1},{3,2},{4,3},{5,4},{6,5},{7,6},{8,7},{9,8},{10,9},{11,1... | collective-permute-start | bytes 98312 | tf_op jit(solution)/shard_map/while/body/eval_jaxpr/ppermute | solution.py:22
  346.3 7.3 %collective-permute-start.1 = (f32[1,16,512]{2,1,0:T(8,128)S(1)}, f32[1,16,512]{2,1,0:T(8,128)S(1)}, u32[]{:S(2)}, u32[]{:S(2)}) collective-permute-start(f32[1,16,512]{2,1,0:T(8,128)S(1)} %get-tuple-element.112), channel_id=1, source_target_pairs={{1,0},{2,1},{3,2},{4,3},{5,4},{6,5},{7,6},{8,7},{9,8},{10,9},{11,1... | collective-permute-start | bytes 98312 | tf_op jit(solution)/shard_map/while/body/eval_jaxpr/ppermute | solution.py:22
  357.7 7.3 %collective-permute-start.1 = (f32[1,16,512]{2,1,0:T(8,128)S(1)}, f32[1,16,512]{2,1,0:T(8,128)S(1)}, u32[]{:S(2)}, u32[]{:S(2)}) collective-permute-start(f32[1,16,512]{2,1,0:T(8,128)S(1)} %get-tuple-element.112), channel_id=1, source_target_pairs={{1,0},{2,1},{3,2},{4,3},{5,4},{6,5},{7,6},{8,7},{9,8},{10,9},{11,1... | collective-permute-start | bytes 98312 | tf_op jit(solution)/shard_map/while/body/eval_jaxpr/ppermute | solution.py:22
  369.0 7.3 %collective-permute-start.1 = (f32[1,16,512]{2,1,0:T(8,128)S(1)}, f32[1,16,512]{2,1,0:T(8,128)S(1)}, u32[]{:S(2)}, u32[]{:S(2)}) collective-permute-start(f32[1,16,512]{2,1,0:T(8,128)S(1)} %get-tuple-element.112), channel_id=1, source_target_pairs={{1,0},{2,1},{3,2},{4,3},{5,4},{6,5},{7,6},{8,7},{9,8},{10,9},{11,1... | collective-permute-start | bytes 98312 | tf_op jit(solution)/shard_map/while/body/eval_jaxpr/ppermute | solution.py:22
  380.4 7.3 %collective-permute-start.1 = (f32[1,16,512]{2,1,0:T(8,128)S(1)}, f32[1,16,512]{2,1,0:T(8,128)S(1)}, u32[]{:S(2)}, u32[]{:S(2)}) collective-permute-start(f32[1,16,512]{2,1,0:T(8,128)S(1)} %get-tuple-element.112), channel_id=1, source_target_pairs={{1,0},{2,1},{3,2},{4,3},{5,4},{6,5},{7,6},{8,7},{9,8},{10,9},{11,1... | collective-permute-start | bytes 98312 | tf_op jit(solution)/shard_map/while/body/eval_jaxpr/ppermute | solution.py:22
  391.7 7.3 %collective-permute-start.1 = (f32[1,16,512]{2,1,0:T(8,128)S(1)}, f32[1,16,512]{2,1,0:T(8,128)S(1)}, u32[]{:S(2)}, u32[]{:S(2)}) collective-permute-start(f32[1,16,512]{2,1,0:T(8,128)S(1)} %get-tuple-element.112), channel_id=1, source_target_pairs={{1,0},{2,1},{3,2},{4,3},{5,4},{6,5},{7,6},{8,7},{9,8},{10,9},{11,1... | collective-permute-start | bytes 98312 | tf_op jit(solution)/shard_map/while/body/eval_jaxpr/ppermute | solution.py:22
  403.1 7.3 %collective-permute-start.1 = (f32[1,16,512]{2,1,0:T(8,128)S(1)}, f32[1,16,512]{2,1,0:T(8,128)S(1)}, u32[]{:S(2)}, u32[]{:S(2)}) collective-permute-start(f32[1,16,512]{2,1,0:T(8,128)S(1)} %get-tuple-element.112), channel_id=1, source_target_pairs={{1,0},{2,1},{3,2},{4,3},{5,4},{6,5},{7,6},{8,7},{9,8},{10,9},{11,1... | collective-permute-start | bytes 98312 | tf_op jit(solution)/shard_map/while/body/eval_jaxpr/ppermute | solution.py:22
  414.5 7.3 %collective-permute-start.1 = (f32[1,16,512]{2,1,0:T(8,128)S(1)}, f32[1,16,512]{2,1,0:T(8,128)S(1)}, u32[]{:S(2)}, u32[]{:S(2)}) collective-permute-start(f32[1,16,512]{2,1,0:T(8,128)S(1)} %get-tuple-element.112), channel_id=1, source_target_pairs={{1,0},{2,1},{3,2},{4,3},{5,4},{6,5},{7,6},{8,7},{9,8},{10,9},{11,1... | collective-permute-start | bytes 98312 | tf_op jit(solution)/shard_map/while/body/eval_jaxpr/ppermute | solution.py:22
  425.8 7.3 %collective-permute-start.1 = (f32[1,16,512]{2,1,0:T(8,128)S(1)}, f32[1,16,512]{2,1,0:T(8,128)S(1)}, u32[]{:S(2)}, u32[]{:S(2)}) collective-permute-start(f32[1,16,512]{2,1,0:T(8,128)S(1)} %get-tuple-element.112), channel_id=1, source_target_pairs={{1,0},{2,1},{3,2},{4,3},{5,4},{6,5},{7,6},{8,7},{9,8},{10,9},{11,1... | collective-permute-start | bytes 98312 | tf_op jit(solution)/shard_map/while/body/eval_jaxpr/ppermute | solution.py:22
  437.2 7.3 %collective-permute-start.1 = (f32[1,16,512]{2,1,0:T(8,128)S(1)}, f32[1,16,512]{2,1,0:T(8,128)S(1)}, u32[]{:S(2)}, u32[]{:S(2)}) collective-permute-start(f32[1,16,512]{2,1,0:T(8,128)S(1)} %get-tuple-element.112), channel_id=1, source_target_pairs={{1,0},{2,1},{3,2},{4,3},{5,4},{6,5},{7,6},{8,7},{9,8},{10,9},{11,1... | collective-permute-start | bytes 98312 | tf_op jit(solution)/shard_map/while/body/eval_jaxpr/ppermute | solution.py:22
  448.5 7.3 %collective-permute-start.1 = (f32[1,16,512]{2,1,0:T(8,128)S(1)}, f32[1,16,512]{2,1,0:T(8,128)S(1)}, u32[]{:S(2)}, u32[]{:S(2)}) collective-permute-start(f32[1,16,512]{2,1,0:T(8,128)S(1)} %get-tuple-element.112), channel_id=1, source_target_pairs={{1,0},{2,1},{3,2},{4,3},{5,4},{6,5},{7,6},{8,7},{9,8},{10,9},{11,1... | collective-permute-start | bytes 98312 | tf_op jit(solution)/shard_map/while/body/eval_jaxpr/ppermute | solution.py:22
  459.9 7.3 %collective-permute-start.1 = (f32[1,16,512]{2,1,0:T(8,128)S(1)}, f32[1,16,512]{2,1,0:T(8,128)S(1)}, u32[]{:S(2)}, u32[]{:S(2)}) collective-permute-start(f32[1,16,512]{2,1,0:T(8,128)S(1)} %get-tuple-element.112), channel_id=1, source_target_pairs={{1,0},{2,1},{3,2},{4,3},{5,4},{6,5},{7,6},{8,7},{9,8},{10,9},{11,1... | collective-permute-start | bytes 98312 | tf_op jit(solution)/shard_map/while/body/eval_jaxpr/ppermute | solution.py:22
  505.1 129.0 %all-reduce.4 = f32[4096]{0:T(1024)S(1)} all-reduce(f32[4096]{0:T(1024)S(1)} %scatter_custom_fusion), channel_id=2, replica_groups=mesh['dir'=16,'space'=32] {'space'}, use_global_device_ids=true, to_apply=%region_4.5.clone | all-reduce | flops 4096 | bytes 32768
  (201 shorter events, 131.6 us)
Async XLA Ops:
  7.2 145.5 %all-gather.2.cloned.1.call-start = ((), (), s32[]{:S(2)}) async-start(), calls=%async_computation | async-start | bytes 1622016 | tf_op jit(solution)/shard_map/all_gather | solution.py:99
  248.5 10.7 %collective-permute-start.2 = (f32[3,2,16,512]{3,2,1,0:T(8,128)S(1)}, f32[3,2,16,512]{3,2,1,0:T(8,128)S(1)}, u32[]{:S(2)}, u32[]{:S(2)}) collective-permute-start(f32[3,2,16,512]{3,2,1,0:T(8,128)S(1)} %get-tuple-element.84), channel_id=1, source_target_pairs={{0,1},{1,2},{2,3},{3,4},{4,5},{5,6},{6,7},{7,8},{8,9},{9,10},{10,1... | collective-permute-start | bytes 589832 | tf_op jit(solution)/shard_map/ppermute | solution.py:20
  250.6 10.3 %collective-permute-start.3 = (f32[3,2,16,512]{3,2,1,0:T(8,128)S(1)}, f32[3,2,16,512]{3,2,1,0:T(8,128)S(1)}, u32[]{:S(2)}, u32[]{:S(2)}) collective-permute-start(f32[3,2,16,512]{3,2,1,0:T(8,128)S(1)} %get-tuple-element.85), channel_id=1, source_target_pairs={{1,0},{2,1},{3,2},{4,3},{5,4},{6,5},{7,6},{8,7},{9,8},{10,9},{11,1... | collective-permute-start | bytes 589832 | tf_op jit(solution)/shard_map/ppermute | solution.py:22
  264.7 9.4 %collective-permute-start = (f32[1,16,512]{2,1,0:T(8,128)S(1)}, f32[1,16,512]{2,1,0:T(8,128)S(1)}, u32[]{:S(2)}, u32[]{:S(2)}) collective-permute-start(f32[1,16,512]{2,1,0:T(8,128)S(1)} %get-tuple-element.111), channel_id=1, source_target_pairs={{0,1},{1,2},{2,3},{3,4},{4,5},{5,6},{6,7},{7,8},{8,9},{9,10},{10,1... | collective-permute-start | bytes 98312 | tf_op jit(solution)/shard_map/while/body/eval_jaxpr/ppermute | solution.py:20
  276.2 9.2 %collective-permute-start = (f32[1,16,512]{2,1,0:T(8,128)S(1)}, f32[1,16,512]{2,1,0:T(8,128)S(1)}, u32[]{:S(2)}, u32[]{:S(2)}) collective-permute-start(f32[1,16,512]{2,1,0:T(8,128)S(1)} %get-tuple-element.111), channel_id=1, source_target_pairs={{0,1},{1,2},{2,3},{3,4},{4,5},{5,6},{6,7},{7,8},{8,9},{9,10},{10,1... | collective-permute-start | bytes 98312 | tf_op jit(solution)/shard_map/while/body/eval_jaxpr/ppermute | solution.py:20
  287.6 9.2 %collective-permute-start = (f32[1,16,512]{2,1,0:T(8,128)S(1)}, f32[1,16,512]{2,1,0:T(8,128)S(1)}, u32[]{:S(2)}, u32[]{:S(2)}) collective-permute-start(f32[1,16,512]{2,1,0:T(8,128)S(1)} %get-tuple-element.111), channel_id=1, source_target_pairs={{0,1},{1,2},{2,3},{3,4},{4,5},{5,6},{6,7},{7,8},{8,9},{9,10},{10,1... | collective-permute-start | bytes 98312 | tf_op jit(solution)/shard_map/while/body/eval_jaxpr/ppermute | solution.py:20
  298.9 9.2 %collective-permute-start = (f32[1,16,512]{2,1,0:T(8,128)S(1)}, f32[1,16,512]{2,1,0:T(8,128)S(1)}, u32[]{:S(2)}, u32[]{:S(2)}) collective-permute-start(f32[1,16,512]{2,1,0:T(8,128)S(1)} %get-tuple-element.111), channel_id=1, source_target_pairs={{0,1},{1,2},{2,3},{3,4},{4,5},{5,6},{6,7},{7,8},{8,9},{9,10},{10,1... | collective-permute-start | bytes 98312 | tf_op jit(solution)/shard_map/while/body/eval_jaxpr/ppermute | solution.py:20
  310.3 9.2 %collective-permute-start = (f32[1,16,512]{2,1,0:T(8,128)S(1)}, f32[1,16,512]{2,1,0:T(8,128)S(1)}, u32[]{:S(2)}, u32[]{:S(2)}) collective-permute-start(f32[1,16,512]{2,1,0:T(8,128)S(1)} %get-tuple-element.111), channel_id=1, source_target_pairs={{0,1},{1,2},{2,3},{3,4},{4,5},{5,6},{6,7},{7,8},{8,9},{9,10},{10,1... | collective-permute-start | bytes 98312 | tf_op jit(solution)/shard_map/while/body/eval_jaxpr/ppermute | solution.py:20
  321.6 9.2 %collective-permute-start = (f32[1,16,512]{2,1,0:T(8,128)S(1)}, f32[1,16,512]{2,1,0:T(8,128)S(1)}, u32[]{:S(2)}, u32[]{:S(2)}) collective-permute-start(f32[1,16,512]{2,1,0:T(8,128)S(1)} %get-tuple-element.111), channel_id=1, source_target_pairs={{0,1},{1,2},{2,3},{3,4},{4,5},{5,6},{6,7},{7,8},{8,9},{9,10},{10,1... | collective-permute-start | bytes 98312 | tf_op jit(solution)/shard_map/while/body/eval_jaxpr/ppermute | solution.py:20
  333.0 9.2 %collective-permute-start = (f32[1,16,512]{2,1,0:T(8,128)S(1)}, f32[1,16,512]{2,1,0:T(8,128)S(1)}, u32[]{:S(2)}, u32[]{:S(2)}) collective-permute-start(f32[1,16,512]{2,1,0:T(8,128)S(1)} %get-tuple-element.111), channel_id=1, source_target_pairs={{0,1},{1,2},{2,3},{3,4},{4,5},{5,6},{6,7},{7,8},{8,9},{9,10},{10,1... | collective-permute-start | bytes 98312 | tf_op jit(solution)/shard_map/while/body/eval_jaxpr/ppermute | solution.py:20
  344.4 9.2 %collective-permute-start = (f32[1,16,512]{2,1,0:T(8,128)S(1)}, f32[1,16,512]{2,1,0:T(8,128)S(1)}, u32[]{:S(2)}, u32[]{:S(2)}) collective-permute-start(f32[1,16,512]{2,1,0:T(8,128)S(1)} %get-tuple-element.111), channel_id=1, source_target_pairs={{0,1},{1,2},{2,3},{3,4},{4,5},{5,6},{6,7},{7,8},{8,9},{9,10},{10,1... | collective-permute-start | bytes 98312 | tf_op jit(solution)/shard_map/while/body/eval_jaxpr/ppermute | solution.py:20
  355.7 9.2 %collective-permute-start = (f32[1,16,512]{2,1,0:T(8,128)S(1)}, f32[1,16,512]{2,1,0:T(8,128)S(1)}, u32[]{:S(2)}, u32[]{:S(2)}) collective-permute-start(f32[1,16,512]{2,1,0:T(8,128)S(1)} %get-tuple-element.111), channel_id=1, source_target_pairs={{0,1},{1,2},{2,3},{3,4},{4,5},{5,6},{6,7},{7,8},{8,9},{9,10},{10,1... | collective-permute-start | bytes 98312 | tf_op jit(solution)/shard_map/while/body/eval_jaxpr/ppermute | solution.py:20
  367.1 9.2 %collective-permute-start = (f32[1,16,512]{2,1,0:T(8,128)S(1)}, f32[1,16,512]{2,1,0:T(8,128)S(1)}, u32[]{:S(2)}, u32[]{:S(2)}) collective-permute-start(f32[1,16,512]{2,1,0:T(8,128)S(1)} %get-tuple-element.111), channel_id=1, source_target_pairs={{0,1},{1,2},{2,3},{3,4},{4,5},{5,6},{6,7},{7,8},{8,9},{9,10},{10,1... | collective-permute-start | bytes 98312 | tf_op jit(solution)/shard_map/while/body/eval_jaxpr/ppermute | solution.py:20
  378.4 9.2 %collective-permute-start = (f32[1,16,512]{2,1,0:T(8,128)S(1)}, f32[1,16,512]{2,1,0:T(8,128)S(1)}, u32[]{:S(2)}, u32[]{:S(2)}) collective-permute-start(f32[1,16,512]{2,1,0:T(8,128)S(1)} %get-tuple-element.111), channel_id=1, source_target_pairs={{0,1},{1,2},{2,3},{3,4},{4,5},{5,6},{6,7},{7,8},{8,9},{9,10},{10,1... | collective-permute-start | bytes 98312 | tf_op jit(solution)/shard_map/while/body/eval_jaxpr/ppermute | solution.py:20
  389.8 9.2 %collective-permute-start = (f32[1,16,512]{2,1,0:T(8,128)S(1)}, f32[1,16,512]{2,1,0:T(8,128)S(1)}, u32[]{:S(2)}, u32[]{:S(2)}) collective-permute-start(f32[1,16,512]{2,1,0:T(8,128)S(1)} %get-tuple-element.111), channel_id=1, source_target_pairs={{0,1},{1,2},{2,3},{3,4},{4,5},{5,6},{6,7},{7,8},{8,9},{9,10},{10,1... | collective-permute-start | bytes 98312 | tf_op jit(solution)/shard_map/while/body/eval_jaxpr/ppermute | solution.py:20
  401.2 9.2 %collective-permute-start = (f32[1,16,512]{2,1,0:T(8,128)S(1)}, f32[1,16,512]{2,1,0:T(8,128)S(1)}, u32[]{:S(2)}, u32[]{:S(2)}) collective-permute-start(f32[1,16,512]{2,1,0:T(8,128)S(1)} %get-tuple-element.111), channel_id=1, source_target_pairs={{0,1},{1,2},{2,3},{3,4},{4,5},{5,6},{6,7},{7,8},{8,9},{9,10},{10,1... | collective-permute-start | bytes 98312 | tf_op jit(solution)/shard_map/while/body/eval_jaxpr/ppermute | solution.py:20
  412.5 9.2 %collective-permute-start = (f32[1,16,512]{2,1,0:T(8,128)S(1)}, f32[1,16,512]{2,1,0:T(8,128)S(1)}, u32[]{:S(2)}, u32[]{:S(2)}) collective-permute-start(f32[1,16,512]{2,1,0:T(8,128)S(1)} %get-tuple-element.111), channel_id=1, source_target_pairs={{0,1},{1,2},{2,3},{3,4},{4,5},{5,6},{6,7},{7,8},{8,9},{9,10},{10,1... | collective-permute-start | bytes 98312 | tf_op jit(solution)/shard_map/while/body/eval_jaxpr/ppermute | solution.py:20
  423.9 9.2 %collective-permute-start = (f32[1,16,512]{2,1,0:T(8,128)S(1)}, f32[1,16,512]{2,1,0:T(8,128)S(1)}, u32[]{:S(2)}, u32[]{:S(2)}) collective-permute-start(f32[1,16,512]{2,1,0:T(8,128)S(1)} %get-tuple-element.111), channel_id=1, source_target_pairs={{0,1},{1,2},{2,3},{3,4},{4,5},{5,6},{6,7},{7,8},{8,9},{9,10},{10,1... | collective-permute-start | bytes 98312 | tf_op jit(solution)/shard_map/while/body/eval_jaxpr/ppermute | solution.py:20
  435.2 9.2 %collective-permute-start = (f32[1,16,512]{2,1,0:T(8,128)S(1)}, f32[1,16,512]{2,1,0:T(8,128)S(1)}, u32[]{:S(2)}, u32[]{:S(2)}) collective-permute-start(f32[1,16,512]{2,1,0:T(8,128)S(1)} %get-tuple-element.111), channel_id=1, source_target_pairs={{0,1},{1,2},{2,3},{3,4},{4,5},{5,6},{6,7},{7,8},{8,9},{9,10},{10,1... | collective-permute-start | bytes 98312 | tf_op jit(solution)/shard_map/while/body/eval_jaxpr/ppermute | solution.py:20
  446.6 9.2 %collective-permute-start = (f32[1,16,512]{2,1,0:T(8,128)S(1)}, f32[1,16,512]{2,1,0:T(8,128)S(1)}, u32[]{:S(2)}, u32[]{:S(2)}) collective-permute-start(f32[1,16,512]{2,1,0:T(8,128)S(1)} %get-tuple-element.111), channel_id=1, source_target_pairs={{0,1},{1,2},{2,3},{3,4},{4,5},{5,6},{6,7},{7,8},{8,9},{9,10},{10,1... | collective-permute-start | bytes 98312 | tf_op jit(solution)/shard_map/while/body/eval_jaxpr/ppermute | solution.py:20
  458.0 9.2 %collective-permute-start = (f32[1,16,512]{2,1,0:T(8,128)S(1)}, f32[1,16,512]{2,1,0:T(8,128)S(1)}, u32[]{:S(2)}, u32[]{:S(2)}) collective-permute-start(f32[1,16,512]{2,1,0:T(8,128)S(1)} %get-tuple-element.111), channel_id=1, source_target_pairs={{0,1},{1,2},{2,3},{3,4},{4,5},{5,6},{6,7},{7,8},{8,9},{9,10},{10,1... | collective-permute-start | bytes 98312 | tf_op jit(solution)/shard_map/while/body/eval_jaxpr/ppermute | solution.py:20
  469.3 9.2 %collective-permute-start = (f32[1,16,512]{2,1,0:T(8,128)S(1)}, f32[1,16,512]{2,1,0:T(8,128)S(1)}, u32[]{:S(2)}, u32[]{:S(2)}) collective-permute-start(f32[1,16,512]{2,1,0:T(8,128)S(1)} %get-tuple-element.111), channel_id=1, source_target_pairs={{0,1},{1,2},{2,3},{3,4},{4,5},{5,6},{6,7},{7,8},{8,9},{9,10},{10,1... | collective-permute-start | bytes 98312 | tf_op jit(solution)/shard_map/while/body/eval_jaxpr/ppermute | solution.py:20
  492.0 142.7 %collective-permute-start.4 = (f32[1,16,512]{2,1,0:T(8,128)S(1)}, f32[1,16,512]{2,1,0:T(8,128)S(1)}, u32[]{:S(2)}, u32[]{:S(2)}) collective-permute-start(f32[1,16,512]{2,1,0:T(8,128)S(1)} %get-tuple-element.88), channel_id=1, source_target_pairs={{0,1},{1,2},{2,3},{3,4},{4,5},{5,6},{6,7},{7,8},{8,9},{9,10},{10,1... | collective-permute-start | bytes 98312 | tf_op jit(solution)/shard_map/ppermute | solution.py:20
  494.1 140.6 %collective-permute-start.5 = (f32[1,16,512]{2,1,0:T(8,128)S(1)}, f32[1,16,512]{2,1,0:T(8,128)S(1)}, u32[]{:S(2)}, u32[]{:S(2)}) collective-permute-start(f32[1,16,512]{2,1,0:T(8,128)S(1)} %get-tuple-element.89), channel_id=1, source_target_pairs={{1,0},{2,1},{3,2},{4,3},{5,4},{6,5},{7,6},{8,7},{9,8},{10,9},{11,1... | collective-permute-start | bytes 98312 | tf_op jit(solution)/shard_map/ppermute | solution.py:22
  (29 other events, 497.2 us)
Sparse Core Ops, SparseCore 0:
  70.7 81.9 all-gather.1
where the time goes:
time: 646 us; the launch traced here: 643 us
  starting transfers between devices  202 us (31%)
  blocking collectives  192 us (30%)
  waiting for transfers between devices  115 us (18%)
  local copies, waits for them, and re-layouts  102 us (16%)
  other arithmetic  16.1 us (2%)
  between operations  15 us (2%)
    ppermute x22, starting transfers between devices, extended_2(): lax.ppermute(head, axis, [((i + 1) % count, i) for i in range(ends)])  160 us
    unnamed x1, blocking collectives  129 us
    all_gather x1, waiting for transfers between devices, body(): plane = lax.all_gather(plane_piece[0], 'space', axis=1, tiled=True)  80 us
    psum x1, blocking collectives, spread(): return lax.psum(block, axis)  62.6 us
    gather x2, local copies, waits for them, and re-layouts, body(): jnp.take(flat_plane, rot_map[0].reshape(-1), axis=1)  62.2 us
    ppermute x22, starting transfers between devices, extended_2(): lax.ppermute(tail, axis, [(i, (i + 1) % count) for i in range(ends)])  42.7 us
    ppermute x22, waiting for transfers between devices, extended_2(): lax.ppermute(head, axis, [((i + 1) % count, i) for i in range(ends)])  33 us
    all_gather x1, local copies, waits for them, and re-layouts, body(): plane = lax.all_gather(plane_piece[0], 'space', axis=1, tiled=True)  32.7 us
  transfers between devices with their start and end apart: 45, of which 23 were waited for; matrix products, arithmetic and copies ran while one was open for 1% of the time, Pallas kernels for 0%

commit v1 on v0

--- a/solution.py
+++ b/solution.py
@@ -28,7 +28,7 @@
 
 def spread(block, axis, holder):
     block = jnp.where(lax.axis_index(axis) == holder, block, jnp.zeros_like(block))
-    return lax.psum(block, axis)
+    return jnp.sum(lax.all_gather(block, axis), axis=0)
 
 
 def pad_edges(field):

time: 646 us -> 620 us (0.960)
  blocking collectives: 192 us -> 165 us
    psum x1 -> x0, blocking collectives: 62.6 us -> none  [spread(): return lax.psum(block, axis)]
    all_gather x0 -> x1, blocking collectives: none -> 36.4 us  [spread(): return jnp.sum(lax.all_gather(block, axis), axis=0)]
where the time goes in v1:
time: 620 us; the launch traced here: 617 us
  starting transfers between devices  202 us (33%)
  blocking collectives  165 us (27%)
  waiting for transfers between devices  114 us (18%)
  local copies, waits for them, and re-layouts  102 us (16%)
  other arithmetic  16.8 us (3%)
  between operations  15 us (2%)
    ppermute x22, starting transfers between devices, extended_2(): lax.ppermute(head, axis, [((i + 1) % count, i) for i in range(ends)])  160 us
    unnamed x1, blocking collectives  129 us
    all_gather x1, waiting for transfers between devices, body(): plane = lax.all_gather(plane_piece[0], 'space', axis=1, tiled=True)  79.9 us
    gather x2, local copies, waits for them, and re-layouts, body(): jnp.take(flat_plane, rot_map[0].reshape(-1), axis=1)  62.2 us
    ppermute x22, starting transfers between devices, extended_2(): lax.ppermute(tail, axis, [(i, (i + 1) % count) for i in range(ends)])  42.7 us
    all_gather x1, blocking collectives, spread(): return jnp.sum(lax.all_gather(block, axis), axis=0)  36.4 us
    ppermute x22, waiting for transfers between devices, extended_2(): lax.ppermute(head, axis, [((i + 1) % count, i) for i in range(ends)])  33 us
    all_gather x1, local copies, waits for them, and re-layouts, body(): plane = lax.all_gather(plane_piece[0], 'space', axis=1, tiled=True)  32.7 us
  transfers between devices with their start and end apart: 45, of which 23 were waited for; matrix products, arithmetic and copies ran while one was open for 1% of the time, Pallas kernels for 0%

profile of v1, /device:TPU:264, one launch (start us, length us, event | category | flops | bytes accessed | tf_op | source)
XLA Modules:
  0.0 617.5 jit_solution(7491330444390694731)
XLA Ops:
  8.0 36.4 %all-gather = f32[16,3,8,512]{3,2,1,0:T(8,128)S(1)} all-gather(f32[1,3,8,512]{3,2,1,0:T(8,128)S(1)} %broadcast_select_fusion.2), channel_id=2, replica_groups=mesh['dir'=16,'space'=32] {'dir'}, dimensions={0}, use_global_device_ids=true | all-gather | bytes 835584 | tf_op jit(solution)/shard_map/all_gather | solution.py:31
  47.1 79.9 %all-gather.3.cloned.1.call-done = f32[3,256,512]{2,1,0:T(8,128)} async-done(((f32[3,8,512]{2,1,0:T(8,128)}), f32[3,256,512]{2,1,0:T(8,128)}) %all-gather.3.cloned.1.call-update) | async-done | bytes 1572880 | tf_op jit(solution)/shard_map/all_gather | solution.py:99
  127.0 32.7 %copy.12 = f32[3,256,512]{0,2,1:T(8,128)} copy(f32[3,256,512]{2,1,0:T(8,128)} %all-gather.3.cloned.1.call-done) | data formatting | bytes 3145728 | tf_op jit(solution)/shard_map/all_gather | solution.py:99
  159.8 60.0 %gather_fusion = f32[4096,3]{1,0:T(8,128)} fusion(f32[3,131072]{0,1:T(8,128)} %bitcast.2, s32[4096]{0:T(1024)S(1)} %broadcast_clamp_fusion), kind=kCustom, calls=%fused_computation | custom fusion | bytes 114688 | tf_op jit(solution)/shard_map/jit(_take)/gather | solution.py:101
  239.0 227.4 %while.14 = (s32[]{:T(128)}, f32[8,16,512]{2,1,0:T(8,128)S(1)}, f32[8,16,512]{2,1,0:T(8,128)S(1)}, s32[]{:T(128)}, s32[]{:T(128)}) while((s32[]{:T(128)}, f32[8,16,512]{2,1,0:T(8,128)S(1)}, f32[8,16,512]{2,1,0:T(8,128)S(1)}, s32[]{:T(128)}, s32[]{:T(128)}) %tuple.48), condition=%wide.region_2.3_spmd.clone, body=%wide.region_1.2_spmd.clone.sunk | while | flops 2108699 | bytes 3515959 | solution.py:117
  241.1 7.3 %collective-permute-start.1 = (f32[1,16,512]{2,1,0:T(8,128)S(1)}, f32[1,16,512]{2,1,0:T(8,128)S(1)}, u32[]{:S(2)}, u32[]{:S(2)}) collective-permute-start(f32[1,16,512]{2,1,0:T(8,128)S(1)} %get-tuple-element.112), channel_id=1, source_target_pairs={{1,0},{2,1},{3,2},{4,3},{5,4},{6,5},{7,6},{8,7},{9,8},{10,9},{11,1... | collective-permute-start | bytes 98312 | tf_op jit(solution)/shard_map/while/body/eval_jaxpr/ppermute | solution.py:22
  252.5 7.3 %collective-permute-start.1 = (f32[1,16,512]{2,1,0:T(8,128)S(1)}, f32[1,16,512]{2,1,0:T(8,128)S(1)}, u32[]{:S(2)}, u32[]{:S(2)}) collective-permute-start(f32[1,16,512]{2,1,0:T(8,128)S(1)} %get-tuple-element.112), channel_id=1, source_target_pairs={{1,0},{2,1},{3,2},{4,3},{5,4},{6,5},{7,6},{8,7},{9,8},{10,9},{11,1... | collective-permute-start | bytes 98312 | tf_op jit(solution)/shard_map/while/body/eval_jaxpr/ppermute | solution.py:22
  263.8 7.3 %collective-permute-start.1 = (f32[1,16,512]{2,1,0:T(8,128)S(1)}, f32[1,16,512]{2,1,0:T(8,128)S(1)}, u32[]{:S(2)}, u32[]{:S(2)}) collective-permute-start(f32[1,16,512]{2,1,0:T(8,128)S(1)} %get-tuple-element.112), channel_id=1, source_target_pairs={{1,0},{2,1},{3,2},{4,3},{5,4},{6,5},{7,6},{8,7},{9,8},{10,9},{11,1... | collective-permute-start | bytes 98312 | tf_op jit(solution)/shard_map/while/body/eval_jaxpr/ppermute | solution.py:22
  275.2 7.3 %collective-permute-start.1 = (f32[1,16,512]{2,1,0:T(8,128)S(1)}, f32[1,16,512]{2,1,0:T(8,128)S(1)}, u32[]{:S(2)}, u32[]{:S(2)}) collective-permute-start(f32[1,16,512]{2,1,0:T(8,128)S(1)} %get-tuple-element.112), channel_id=1, source_target_pairs={{1,0},{2,1},{3,2},{4,3},{5,4},{6,5},{7,6},{8,7},{9,8},{10,9},{11,1... | collective-permute-start | bytes 98312 | tf_op jit(solution)/shard_map/while/body/eval_jaxpr/ppermute | solution.py:22
  286.6 7.3 %collective-permute-start.1 = (f32[1,16,512]{2,1,0:T(8,128)S(1)}, f32[1,16,512]{2,1,0:T(8,128)S(1)}, u32[]{:S(2)}, u32[]{:S(2)}) collective-permute-start(f32[1,16,512]{2,1,0:T(8,128)S(1)} %get-tuple-element.112), channel_id=1, source_target_pairs={{1,0},{2,1},{3,2},{4,3},{5,4},{6,5},{7,6},{8,7},{9,8},{10,9},{11,1... | collective-permute-start | bytes 98312 | tf_op jit(solution)/shard_map/while/body/eval_jaxpr/ppermute | solution.py:22
  297.9 7.3 %collective-permute-start.1 = (f32[1,16,512]{2,1,0:T(8,128)S(1)}, f32[1,16,512]{2,1,0:T(8,128)S(1)}, u32[]{:S(2)}, u32[]{:S(2)}) collective-permute-start(f32[1,16,512]{2,1,0:T(8,128)S(1)} %get-tuple-element.112), channel_id=1, source_target_pairs={{1,0},{2,1},{3,2},{4,3},{5,4},{6,5},{7,6},{8,7},{9,8},{10,9},{11,1... | collective-permute-start | bytes 98312 | tf_op jit(solution)/shard_map/while/body/eval_jaxpr/ppermute | solution.py:22
  309.3 7.3 %collective-permute-start.1 = (f32[1,16,512]{2,1,0:T(8,128)S(1)}, f32[1,16,512]{2,1,0:T(8,128)S(1)}, u32[]{:S(2)}, u32[]{:S(2)}) collective-permute-start(f32[1,16,512]{2,1,0:T(8,128)S(1)} %get-tuple-element.112), channel_id=1, source_target_pairs={{1,0},{2,1},{3,2},{4,3},{5,4},{6,5},{7,6},{8,7},{9,8},{10,9},{11,1... | collective-permute-start | bytes 98312 | tf_op jit(solution)/shard_map/while/body/eval_jaxpr/ppermute | solution.py:22
  320.6 7.3 %collective-permute-start.1 = (f32[1,16,512]{2,1,0:T(8,128)S(1)}, f32[1,16,512]{2,1,0:T(8,128)S(1)}, u32[]{:S(2)}, u32[]{:S(2)}) collective-permute-start(f32[1,16,512]{2,1,0:T(8,128)S(1)} %get-tuple-element.112), channel_id=1, source_target_pairs={{1,0},{2,1},{3,2},{4,3},{5,4},{6,5},{7,6},{8,7},{9,8},{10,9},{11,1... | collective-permute-start | bytes 98312 | tf_op jit(solution)/shard_map/while/body/eval_jaxpr/ppermute | solution.py:22
  332.0 7.3 %collective-permute-start.1 = (f32[1,16,512]{2,1,0:T(8,128)S(1)}, f32[1,16,512]{2,1,0:T(8,128)S(1)}, u32[]{:S(2)}, u32[]{:S(2)}) collective-permute-start(f32[1,16,512]{2,1,0:T(8,128)S(1)} %get-tuple-element.112), channel_id=1, source_target_pairs={{1,0},{2,1},{3,2},{4,3},{5,4},{6,5},{7,6},{8,7},{9,8},{10,9},{11,1... | collective-permute-start | bytes 98312 | tf_op jit(solution)/shard_map/while/body/eval_jaxpr/ppermute | solution.py:22
  343.4 7.3 %collective-permute-start.1 = (f32[1,16,512]{2,1,0:T(8,128)S(1)}, f32[1,16,512]{2,1,0:T(8,128)S(1)}, u32[]{:S(2)}, u32[]{:S(2)}) collective-permute-start(f32[1,16,512]{2,1,0:T(8,128)S(1)} %get-tuple-element.112), channel_id=1, source_target_pairs={{1,0},{2,1},{3,2},{4,3},{5,4},{6,5},{7,6},{8,7},{9,8},{10,9},{11,1... | collective-permute-start | bytes 98312 | tf_op jit(solution)/shard_map/while/body/eval_jaxpr/ppermute | solution.py:22
  354.7 7.3 %collective-permute-start.1 = (f32[1,16,512]{2,1,0:T(8,128)S(1)}, f32[1,16,512]{2,1,0:T(8,128)S(1)}, u32[]{:S(2)}, u32[]{:S(2)}) collective-permute-start(f32[1,16,512]{2,1,0:T(8,128)S(1)} %get-tuple-element.112), channel_id=1, source_target_pairs={{1,0},{2,1},{3,2},{4,3},{5,4},{6,5},{7,6},{8,7},{9,8},{10,9},{11,1... | collective-permute-start | bytes 98312 | tf_op jit(solution)/shard_map/while/body/eval_jaxpr/ppermute | solution.py:22
  366.1 7.3 %collective-permute-start.1 = (f32[1,16,512]{2,1,0:T(8,128)S(1)}, f32[1,16,512]{2,1,0:T(8,128)S(1)}, u32[]{:S(2)}, u32[]{:S(2)}) collective-permute-start(f32[1,16,512]{2,1,0:T(8,128)S(1)} %get-tuple-element.112), channel_id=1, source_target_pairs={{1,0},{2,1},{3,2},{4,3},{5,4},{6,5},{7,6},{8,7},{9,8},{10,9},{11,1... | collective-permute-start | bytes 98312 | tf_op jit(solution)/shard_map/while/body/eval_jaxpr/ppermute | solution.py:22
  377.4 7.3 %collective-permute-start.1 = (f32[1,16,512]{2,1,0:T(8,128)S(1)}, f32[1,16,512]{2,1,0:T(8,128)S(1)}, u32[]{:S(2)}, u32[]{:S(2)}) collective-permute-start(f32[1,16,512]{2,1,0:T(8,128)S(1)} %get-tuple-element.112), channel_id=1, source_target_pairs={{1,0},{2,1},{3,2},{4,3},{5,4},{6,5},{7,6},{8,7},{9,8},{10,9},{11,1... | collective-permute-start | bytes 98312 | tf_op jit(solution)/shard_map/while/body/eval_jaxpr/ppermute | solution.py:22
  388.8 7.3 %collective-permute-start.1 = (f32[1,16,512]{2,1,0:T(8,128)S(1)}, f32[1,16,512]{2,1,0:T(8,128)S(1)}, u32[]{:S(2)}, u32[]{:S(2)}) collective-permute-start(f32[1,16,512]{2,1,0:T(8,128)S(1)} %get-tuple-element.112), channel_id=1, source_target_pairs={{1,0},{2,1},{3,2},{4,3},{5,4},{6,5},{7,6},{8,7},{9,8},{10,9},{11,1... | collective-permute-start | bytes 98312 | tf_op jit(solution)/shard_map/while/body/eval_jaxpr/ppermute | solution.py:22
  400.2 7.3 %collective-permute-start.1 = (f32[1,16,512]{2,1,0:T(8,128)S(1)}, f32[1,16,512]{2,1,0:T(8,128)S(1)}, u32[]{:S(2)}, u32[]{:S(2)}) collective-permute-start(f32[1,16,512]{2,1,0:T(8,128)S(1)} %get-tuple-element.112), channel_id=1, source_target_pairs={{1,0},{2,1},{3,2},{4,3},{5,4},{6,5},{7,6},{8,7},{9,8},{10,9},{11,1... | collective-permute-start | bytes 98312 | tf_op jit(solution)/shard_map/while/body/eval_jaxpr/ppermute | solution.py:22
  411.5 7.3 %collective-permute-start.1 = (f32[1,16,512]{2,1,0:T(8,128)S(1)}, f32[1,16,512]{2,1,0:T(8,128)S(1)}, u32[]{:S(2)}, u32[]{:S(2)}) collective-permute-start(f32[1,16,512]{2,1,0:T(8,128)S(1)} %get-tuple-element.112), channel_id=1, source_target_pairs={{1,0},{2,1},{3,2},{4,3},{5,4},{6,5},{7,6},{8,7},{9,8},{10,9},{11,1... | collective-permute-start | bytes 98312 | tf_op jit(solution)/shard_map/while/body/eval_jaxpr/ppermute | solution.py:22
  422.9 7.3 %collective-permute-start.1 = (f32[1,16,512]{2,1,0:T(8,128)S(1)}, f32[1,16,512]{2,1,0:T(8,128)S(1)}, u32[]{:S(2)}, u32[]{:S(2)}) collective-permute-start(f32[1,16,512]{2,1,0:T(8,128)S(1)} %get-tuple-element.112), channel_id=1, source_target_pairs={{1,0},{2,1},{3,2},{4,3},{5,4},{6,5},{7,6},{8,7},{9,8},{10,9},{11,1... | collective-permute-start | bytes 98312 | tf_op jit(solution)/shard_map/while/body/eval_jaxpr/ppermute | solution.py:22
  434.2 7.3 %collective-permute-start.1 = (f32[1,16,512]{2,1,0:T(8,128)S(1)}, f32[1,16,512]{2,1,0:T(8,128)S(1)}, u32[]{:S(2)}, u32[]{:S(2)}) collective-permute-start(f32[1,16,512]{2,1,0:T(8,128)S(1)} %get-tuple-element.112), channel_id=1, source_target_pairs={{1,0},{2,1},{3,2},{4,3},{5,4},{6,5},{7,6},{8,7},{9,8},{10,9},{11,1... | collective-permute-start | bytes 98312 | tf_op jit(solution)/shard_map/while/body/eval_jaxpr/ppermute | solution.py:22
  479.5 129.0 %all-reduce.4 = f32[4096]{0:T(1024)S(1)} all-reduce(f32[4096]{0:T(1024)S(1)} %scatter_custom_fusion), channel_id=3, replica_groups=mesh['dir'=16,'space'=32] {'space'}, use_global_device_ids=true, to_apply=%region_4.5.clone | all-reduce | flops 4096 | bytes 32768
  (202 shorter events, 132.3 us)
Async XLA Ops:
  7.2 119.9 %all-gather.3.cloned.1.call-start = ((), (), s32[]{:S(2)}) async-start(), calls=%async_computation | async-start | bytes 1622016 | tf_op jit(solution)/shard_map/all_gather | solution.py:99
  222.9 10.7 %collective-permute-start.2 = (f32[3,2,16,512]{3,2,1,0:T(8,128)S(1)}, f32[3,2,16,512]{3,2,1,0:T(8,128)S(1)}, u32[]{:S(2)}, u32[]{:S(2)}) collective-permute-start(f32[3,2,16,512]{3,2,1,0:T(8,128)S(1)} %get-tuple-element.84), channel_id=1, source_target_pairs={{0,1},{1,2},{2,3},{3,4},{4,5},{5,6},{6,7},{7,8},{8,9},{9,10},{10,1... | collective-permute-start | bytes 589832 | tf_op jit(solution)/shard_map/ppermute | solution.py:20
  224.9 10.3 %collective-permute-start.3 = (f32[3,2,16,512]{3,2,1,0:T(8,128)S(1)}, f32[3,2,16,512]{3,2,1,0:T(8,128)S(1)}, u32[]{:S(2)}, u32[]{:S(2)}) collective-permute-start(f32[3,2,16,512]{3,2,1,0:T(8,128)S(1)} %get-tuple-element.85), channel_id=1, source_target_pairs={{1,0},{2,1},{3,2},{4,3},{5,4},{6,5},{7,6},{8,7},{9,8},{10,9},{11,1... | collective-permute-start | bytes 589832 | tf_op jit(solution)/shard_map/ppermute | solution.py:22
  239.0 9.4 %collective-permute-start = (f32[1,16,512]{2,1,0:T(8,128)S(1)}, f32[1,16,512]{2,1,0:T(8,128)S(1)}, u32[]{:S(2)}, u32[]{:S(2)}) collective-permute-start(f32[1,16,512]{2,1,0:T(8,128)S(1)} %get-tuple-element.111), channel_id=1, source_target_pairs={{0,1},{1,2},{2,3},{3,4},{4,5},{5,6},{6,7},{7,8},{8,9},{9,10},{10,1... | collective-permute-start | bytes 98312 | tf_op jit(solution)/shard_map/while/body/eval_jaxpr/ppermute | solution.py:20
  250.5 9.2 %collective-permute-start = (f32[1,16,512]{2,1,0:T(8,128)S(1)}, f32[1,16,512]{2,1,0:T(8,128)S(1)}, u32[]{:S(2)}, u32[]{:S(2)}) collective-permute-start(f32[1,16,512]{2,1,0:T(8,128)S(1)} %get-tuple-element.111), channel_id=1, source_target_pairs={{0,1},{1,2},{2,3},{3,4},{4,5},{5,6},{6,7},{7,8},{8,9},{9,10},{10,1... | collective-permute-start | bytes 98312 | tf_op jit(solution)/shard_map/while/body/eval_jaxpr/ppermute | solution.py:20
  261.9 9.2 %collective-permute-start = (f32[1,16,512]{2,1,0:T(8,128)S(1)}, f32[1,16,512]{2,1,0:T(8,128)S(1)}, u32[]{:S(2)}, u32[]{:S(2)}) collective-permute-start(f32[1,16,512]{2,1,0:T(8,128)S(1)} %get-tuple-element.111), channel_id=1, source_target_pairs={{0,1},{1,2},{2,3},{3,4},{4,5},{5,6},{6,7},{7,8},{8,9},{9,10},{10,1... | collective-permute-start | bytes 98312 | tf_op jit(solution)/shard_map/while/body/eval_jaxpr/ppermute | solution.py:20
  273.3 9.2 %collective-permute-start = (f32[1,16,512]{2,1,0:T(8,128)S(1)}, f32[1,16,512]{2,1,0:T(8,128)S(1)}, u32[]{:S(2)}, u32[]{:S(2)}) collective-permute-start(f32[1,16,512]{2,1,0:T(8,128)S(1)} %get-tuple-element.111), channel_id=1, source_target_pairs={{0,1},{1,2},{2,3},{3,4},{4,5},{5,6},{6,7},{7,8},{8,9},{9,10},{10,1... | collective-permute-start | bytes 98312 | tf_op jit(solution)/shard_map/while/body/eval_jaxpr/ppermute | solution.py:20
  284.6 9.2 %collective-permute-start = (f32[1,16,512]{2,1,0:T(8,128)S(1)}, f32[1,16,512]{2,1,0:T(8,128)S(1)}, u32[]{:S(2)}, u32[]{:S(2)}) collective-permute-start(f32[1,16,512]{2,1,0:T(8,128)S(1)} %get-tuple-element.111), channel_id=1, source_target_pairs={{0,1},{1,2},{2,3},{3,4},{4,5},{5,6},{6,7},{7,8},{8,9},{9,10},{10,1... | collective-permute-start | bytes 98312 | tf_op jit(solution)/shard_map/while/body/eval_jaxpr/ppermute | solution.py:20
  296.0 9.2 %collective-permute-start = (f32[1,16,512]{2,1,0:T(8,128)S(1)}, f32[1,16,512]{2,1,0:T(8,128)S(1)}, u32[]{:S(2)}, u32[]{:S(2)}) collective-permute-start(f32[1,16,512]{2,1,0:T(8,128)S(1)} %get-tuple-element.111), channel_id=1, source_target_pairs={{0,1},{1,2},{2,3},{3,4},{4,5},{5,6},{6,7},{7,8},{8,9},{9,10},{10,1... | collective-permute-start | bytes 98312 | tf_op jit(solution)/shard_map/while/body/eval_jaxpr/ppermute | solution.py:20
  307.3 9.2 %collective-permute-start = (f32[1,16,512]{2,1,0:T(8,128)S(1)}, f32[1,16,512]{2,1,0:T(8,128)S(1)}, u32[]{:S(2)}, u32[]{:S(2)}) collective-permute-start(f32[1,16,512]{2,1,0:T(8,128)S(1)} %get-tuple-element.111), channel_id=1, source_target_pairs={{0,1},{1,2},{2,3},{3,4},{4,5},{5,6},{6,7},{7,8},{8,9},{9,10},{10,1... | collective-permute-start | bytes 98312 | tf_op jit(solution)/shard_map/while/body/eval_jaxpr/ppermute | solution.py:20
  318.7 9.2 %collective-permute-start = (f32[1,16,512]{2,1,0:T(8,128)S(1)}, f32[1,16,512]{2,1,0:T(8,128)S(1)}, u32[]{:S(2)}, u32[]{:S(2)}) collective-permute-start(f32[1,16,512]{2,1,0:T(8,128)S(1)} %get-tuple-element.111), channel_id=1, source_target_pairs={{0,1},{1,2},{2,3},{3,4},{4,5},{5,6},{6,7},{7,8},{8,9},{9,10},{10,1... | collective-permute-start | bytes 98312 | tf_op jit(solution)/shard_map/while/body/eval_jaxpr/ppermute | solution.py:20
  330.1 9.2 %collective-permute-start = (f32[1,16,512]{2,1,0:T(8,128)S(1)}, f32[1,16,512]{2,1,0:T(8,128)S(1)}, u32[]{:S(2)}, u32[]{:S(2)}) collective-permute-start(f32[1,16,512]{2,1,0:T(8,128)S(1)} %get-tuple-element.111), channel_id=1, source_target_pairs={{0,1},{1,2},{2,3},{3,4},{4,5},{5,6},{6,7},{7,8},{8,9},{9,10},{10,1... | collective-permute-start | bytes 98312 | tf_op jit(solution)/shard_map/while/body/eval_jaxpr/ppermute | solution.py:20
  341.4 9.2 %collective-permute-start = (f32[1,16,512]{2,1,0:T(8,128)S(1)}, f32[1,16,512]{2,1,0:T(8,128)S(1)}, u32[]{:S(2)}, u32[]{:S(2)}) collective-permute-start(f32[1,16,512]{2,1,0:T(8,128)S(1)} %get-tuple-element.111), channel_id=1, source_target_pairs={{0,1},{1,2},{2,3},{3,4},{4,5},{5,6},{6,7},{7,8},{8,9},{9,10},{10,1... | collective-permute-start | bytes 98312 | tf_op jit(solution)/shard_map/while/body/eval_jaxpr/ppermute | solution.py:20
  352.8 9.2 %collective-permute-start = (f32[1,16,512]{2,1,0:T(8,128)S(1)}, f32[1,16,512]{2,1,0:T(8,128)S(1)}, u32[]{:S(2)}, u32[]{:S(2)}) collective-permute-start(f32[1,16,512]{2,1,0:T(8,128)S(1)} %get-tuple-element.111), channel_id=1, source_target_pairs={{0,1},{1,2},{2,3},{3,4},{4,5},{5,6},{6,7},{7,8},{8,9},{9,10},{10,1... | collective-permute-start | bytes 98312 | tf_op jit(solution)/shard_map/while/body/eval_jaxpr/ppermute | solution.py:20
  364.1 9.2 %collective-permute-start = (f32[1,16,512]{2,1,0:T(8,128)S(1)}, f32[1,16,512]{2,1,0:T(8,128)S(1)}, u32[]{:S(2)}, u32[]{:S(2)}) collective-permute-start(f32[1,16,512]{2,1,0:T(8,128)S(1)} %get-tuple-element.111), channel_id=1, source_target_pairs={{0,1},{1,2},{2,3},{3,4},{4,5},{5,6},{6,7},{7,8},{8,9},{9,10},{10,1... | collective-permute-start | bytes 98312 | tf_op jit(solution)/shard_map/while/body/eval_jaxpr/ppermute | solution.py:20
  375.5 9.2 %collective-permute-start = (f32[1,16,512]{2,1,0:T(8,128)S(1)}, f32[1,16,512]{2,1,0:T(8,128)S(1)}, u32[]{:S(2)}, u32[]{:S(2)}) collective-permute-start(f32[1,16,512]{2,1,0:T(8,128)S(1)} %get-tuple-element.111), channel_id=1, source_target_pairs={{0,1},{1,2},{2,3},{3,4},{4,5},{5,6},{6,7},{7,8},{8,9},{9,10},{10,1... | collective-permute-start | bytes 98312 | tf_op jit(solution)/shard_map/while/body/eval_jaxpr/ppermute | solution.py:20
  386.9 9.2 %collective-permute-start = (f32[1,16,512]{2,1,0:T(8,128)S(1)}, f32[1,16,512]{2,1,0:T(8,128)S(1)}, u32[]{:S(2)}, u32[]{:S(2)}) collective-permute-start(f32[1,16,512]{2,1,0:T(8,128)S(1)} %get-tuple-element.111), channel_id=1, source_target_pairs={{0,1},{1,2},{2,3},{3,4},{4,5},{5,6},{6,7},{7,8},{8,9},{9,10},{10,1... | collective-permute-start | bytes 98312 | tf_op jit(solution)/shard_map/while/body/eval_jaxpr/ppermute | solution.py:20
  398.2 9.2 %collective-permute-start = (f32[1,16,512]{2,1,0:T(8,128)S(1)}, f32[1,16,512]{2,1,0:T(8,128)S(1)}, u32[]{:S(2)}, u32[]{:S(2)}) collective-permute-start(f32[1,16,512]{2,1,0:T(8,128)S(1)} %get-tuple-element.111), channel_id=1, source_target_pairs={{0,1},{1,2},{2,3},{3,4},{4,5},{5,6},{6,7},{7,8},{8,9},{9,10},{10,1... | collective-permute-start | bytes 98312 | tf_op jit(solution)/shard_map/while/body/eval_jaxpr/ppermute | solution.py:20
  409.6 9.2 %collective-permute-start = (f32[1,16,512]{2,1,0:T(8,128)S(1)}, f32[1,16,512]{2,1,0:T(8,128)S(1)}, u32[]{:S(2)}, u32[]{:S(2)}) collective-permute-start(f32[1,16,512]{2,1,0:T(8,128)S(1)} %get-tuple-element.111), channel_id=1, source_target_pairs={{0,1},{1,2},{2,3},{3,4},{4,5},{5,6},{6,7},{7,8},{8,9},{9,10},{10,1... | collective-permute-start | bytes 98312 | tf_op jit(solution)/shard_map/while/body/eval_jaxpr/ppermute | solution.py:20
  420.9 9.2 %collective-permute-start = (f32[1,16,512]{2,1,0:T(8,128)S(1)}, f32[1,16,512]{2,1,0:T(8,128)S(1)}, u32[]{:S(2)}, u32[]{:S(2)}) collective-permute-start(f32[1,16,512]{2,1,0:T(8,128)S(1)} %get-tuple-element.111), channel_id=1, source_target_pairs={{0,1},{1,2},{2,3},{3,4},{4,5},{5,6},{6,7},{7,8},{8,9},{9,10},{10,1... | collective-permute-start | bytes 98312 | tf_op jit(solution)/shard_map/while/body/eval_jaxpr/ppermute | solution.py:20
  432.3 9.2 %collective-permute-start = (f32[1,16,512]{2,1,0:T(8,128)S(1)}, f32[1,16,512]{2,1,0:T(8,128)S(1)}, u32[]{:S(2)}, u32[]{:S(2)}) collective-permute-start(f32[1,16,512]{2,1,0:T(8,128)S(1)} %get-tuple-element.111), channel_id=1, source_target_pairs={{0,1},{1,2},{2,3},{3,4},{4,5},{5,6},{6,7},{7,8},{8,9},{9,10},{10,1... | collective-permute-start | bytes 98312 | tf_op jit(solution)/shard_map/while/body/eval_jaxpr/ppermute | solution.py:20
  443.7 9.2 %collective-permute-start = (f32[1,16,512]{2,1,0:T(8,128)S(1)}, f32[1,16,512]{2,1,0:T(8,128)S(1)}, u32[]{:S(2)}, u32[]{:S(2)}) collective-permute-start(f32[1,16,512]{2,1,0:T(8,128)S(1)} %get-tuple-element.111), channel_id=1, source_target_pairs={{0,1},{1,2},{2,3},{3,4},{4,5},{5,6},{6,7},{7,8},{8,9},{9,10},{10,1... | collective-permute-start | bytes 98312 | tf_op jit(solution)/shard_map/while/body/eval_jaxpr/ppermute | solution.py:20
  466.4 142.7 %collective-permute-start.4 = (f32[1,16,512]{2,1,0:T(8,128)S(1)}, f32[1,16,512]{2,1,0:T(8,128)S(1)}, u32[]{:S(2)}, u32[]{:S(2)}) collective-permute-start(f32[1,16,512]{2,1,0:T(8,128)S(1)} %get-tuple-element.88), channel_id=1, source_target_pairs={{0,1},{1,2},{2,3},{3,4},{4,5},{5,6},{6,7},{7,8},{8,9},{9,10},{10,1... | collective-permute-start | bytes 98312 | tf_op jit(solution)/shard_map/ppermute | solution.py:20
  468.4 140.6 %collective-permute-start.5 = (f32[1,16,512]{2,1,0:T(8,128)S(1)}, f32[1,16,512]{2,1,0:T(8,128)S(1)}, u32[]{:S(2)}, u32[]{:S(2)}) collective-permute-start(f32[1,16,512]{2,1,0:T(8,128)S(1)} %get-tuple-element.89), channel_id=1, source_target_pairs={{1,0},{2,1},{3,2},{4,3},{5,4},{6,5},{7,6},{8,7},{9,8},{10,9},{11,1... | collective-permute-start | bytes 98312 | tf_op jit(solution)/shard_map/ppermute | solution.py:22
  (29 other events, 446.0 us)
Sparse Core Ops, SparseCore 0:
  45.1 81.8 all-gather.2
